TPU v7x, 32 devices: a whole 2x2x4 slice. The times are simulated.
32 devices in a mesh: section: 4 (over z), ctx: 2 (over x), tp: 4 (over y, core).
Axes of the slice: x: 2, y: 2, z: 4, core: 2. Of those that a mesh axis runs over, the one named last changes fastest.
Arguments:
- block_order: int32 [4], replicated, may hold values from 0 to 3, each once
- plan: int32 [4], replicated, may hold values from 0 to 1
- q_box: bfloat16 [4, 2, 352, 8192], P('section', None, 'ctx', 'tp'), may hold values from -8 to 8
- k_box: bfloat16 [4, 2, 352, 1024], P('section', None, ('ctx', 'tp')), may hold values from -8 to 8
- v_box: bfloat16 [4, 2, 352, 1024], P('section', None, ('ctx', 'tp')), may hold values from -6 to 6
- grad_out: bfloat16 [4, 352, 8192], P('section', 'ctx', 'tp'), may hold values from -6 to 6
Outputs:
- attn_out: bfloat16 [4, 352, 8192], P('section', 'ctx', 'tp')
- grad_q: bfloat16 [4, 352, 8192], P('section', 'ctx', 'tp')
- grad_k: float32 [4, 352, 1024], P('section', ('ctx', 'tp'))
- grad_v: float32 [4, 352, 1024], P('section', ('ctx', 'tp'))
Inputs may be any that keep to these rules, and one draw needn't show every extreme that they name: `block_order`: a permutation: every block sits in exactly one storage slot, slot j covering storage rows j * 88 to (j + 1) * 88 - 1.
All inputs are finite; a program needn't handle non-finite values.
Results may differ from a plain program's by a relative error of at most 0.012.
Values may be sent and summed in bfloat16 or wider, within the bound.
A program may use at most 64 MiB of HBM per device.

v0:
```python
import jax
import jax.numpy as jnp
from jax import lax
from jax.sharding import PartitionSpec as P

HEAD_DIM = 128


NEG = -1e30


def passed_along(block, axis, distance):
    devices = range(lax.axis_size(axis))
    route = [((i - distance) % len(devices), i) for i in devices]
    return lax.ppermute(block, axis, route)


def body(block_order, plan, q_box, k_box, v_box, grad_out):
    tp_count = lax.axis_size("tp")
    ctx_count = lax.axis_size("ctx")
    tok_rows = q_box.shape[2]
    seq_rows = tok_rows * ctx_count
    block_len = tok_rows // 2
    head_size = HEAD_DIM
    heads_local = q_box.shape[3] // head_size
    kv_local = k_box.shape[3] // head_size // tp_count
    group = heads_local // kv_local
    kv_width = kv_local * head_size
    scale = head_size ** (-0.5)
    section_rank = lax.axis_index("section")
    tp_rank = lax.axis_index("tp")
    arrived = passed_along((q_box[0], k_box[0], v_box[0]), "section", 1)
    wanted = lax.dynamic_index_in_dim(plan, section_rank, 0, keepdims=False)
    queries = lax.dynamic_index_in_dim(arrived[0], wanted, 0, keepdims=False)
    key_rows = lax.dynamic_index_in_dim(arrived[1], wanted, 0, keepdims=False)
    value_rows = lax.dynamic_index_in_dim(arrived[2], wanted, 0, keepdims=False)
    cotangent = passed_along(grad_out[0], "section", -1)
    positions = (
        block_order[:, None] * block_len + jnp.arange(block_len, dtype=jnp.int32)[None, :]
    ).reshape(seq_rows)
    query_pos = lax.dynamic_slice_in_dim(positions, lax.axis_index("ctx") * tok_rows, tok_rows)
    key_full, value_full = (
        lax.all_gather(key_rows, ("ctx", "tp"), axis=0, tiled=True),
        lax.all_gather(value_rows, ("ctx", "tp"), axis=0, tiled=True),
    )
    key_store = lax.dynamic_slice_in_dim(key_full, tp_rank * kv_width, kv_width, 1)
    value_store = lax.dynamic_slice_in_dim(value_full, tp_rank * kv_width, kv_width, 1)
    q_split = queries.reshape(tok_rows, kv_local, group, head_size).transpose(1, 2, 0, 3)
    do_split = cotangent.reshape(tok_rows, kv_local, group, head_size).transpose(1, 2, 0, 3)
    key_split = key_store.reshape(seq_rows, kv_local, head_size).transpose(1, 0, 2)
    value_split = value_store.reshape(seq_rows, kv_local, head_size).transpose(1, 0, 2)
    visible_all = positions[None, :] <= query_pos[:, None]

    def per_group(inputs):
        q_group, do_group, key_head, value_head = inputs

        def per_head(sums, head_inputs):
            key_grad, value_grad = sums
            q_one, do_one = head_inputs
            scores = jnp.dot(q_one, key_head.T, preferred_element_type=jnp.float32) * scale
            scores = jnp.where(visible_all, scores, NEG)
            top_score = jnp.max(scores, axis=1, keepdims=True)
            totals = jnp.sum(
                jnp.where(visible_all, jnp.exp(scores - top_score), 0.0), axis=1, keepdims=True
            )
            log_total = top_score + jnp.log(totals)
            probs = jnp.where(visible_all, jnp.exp(scores - log_total), 0.0)
            probs_low = probs.astype(jnp.bfloat16)
            attended = jnp.dot(probs_low, value_head, preferred_element_type=jnp.float32)
            delta = jnp.sum(do_one.astype(jnp.float32) * attended, axis=1, keepdims=True)
            dprobs = jnp.dot(do_one, value_head.T, preferred_element_type=jnp.float32)
            dscores = (probs * (dprobs - delta)).astype(jnp.bfloat16)
            q_grad = (
                jnp.dot(dscores, key_head, preferred_element_type=jnp.float32) * scale
            ).astype(jnp.bfloat16)
            key_grad = (
                key_grad + jnp.dot(dscores.T, q_one, preferred_element_type=jnp.float32) * scale
            )
            value_grad = value_grad + jnp.dot(
                probs_low.T, do_one, preferred_element_type=jnp.float32
            )
            return ((key_grad, value_grad), (attended.astype(jnp.bfloat16), q_grad))

        zero_rows = jnp.zeros((seq_rows, head_size), jnp.float32)
        (key_grad, value_grad), (attended, q_grad) = lax.scan(
            per_head, (zero_rows, zero_rows), (q_group, do_group)
        )
        return (attended, q_grad, key_grad, value_grad)

    attended, q_grad, key_grad, value_grad = lax.map(
        per_group, (q_split, do_split, key_split, value_split)
    )
    attended_flat = attended.transpose(2, 0, 1, 3).reshape(tok_rows, heads_local * head_size)
    q_grad_flat = q_grad.transpose(2, 0, 1, 3).reshape(tok_rows, heads_local * head_size)
    key_terms = key_grad.transpose(1, 0, 2).reshape(seq_rows, kv_width)
    value_terms = value_grad.transpose(1, 0, 2).reshape(seq_rows, kv_width)
    grad_terms = jnp.concatenate([key_terms, value_terms], axis=1)
    own_grads = lax.psum_scatter(grad_terms, "ctx", scatter_dimension=0, tiled=True)
    key_part = own_grads[:, :kv_width]
    value_part = own_grads[:, kv_width:]
    k_grad_tokens, v_grad_tokens = (
        lax.all_to_all(key_part, "tp", split_axis=0, concat_axis=1, tiled=True),
        lax.all_to_all(value_part, "tp", split_axis=0, concat_axis=1, tiled=True),
    )
    return (attended_flat[None], q_grad_flat[None], k_grad_tokens[None], v_grad_tokens[None])


def solution(mesh):
    in_specs = (
        P(),
        P(),
        P("section", None, "ctx", "tp"),
        P("section", None, ("ctx", "tp"), None),
        P("section", None, ("ctx", "tp"), None),
        P("section", "ctx", "tp"),
    )
    out_specs = (
        P("section", "ctx", "tp"),
        P("section", "ctx", "tp"),
        P("section", ("ctx", "tp"), None),
        P("section", ("ctx", "tp"), None),
    )
    return jax.shard_map(body, mesh=mesh, in_specs=in_specs, out_specs=out_specs, check_vma=False)
```

profile of v0, /device:TPU:0, one launch (start us, length us, event | category | flops | bytes accessed | tf_op | source)
XLA Modules:
  0.0 181.7 jit_solution(14124188737722238719)
XLA Ops:
  7.2 3.1 %collective-permute-start = (bf16[2,176,2048]{2,1,0:T(8,128)(2,1)}, bf16[2,176,2048]{2,1,0:T(8,128)(2,1)S(1)}, u32[]{:S(2)}, u32[]{:S(2)}) collective-permute-start(bf16[2,176,2048]{2,1,0:T(8,128)(2,1)} %bitcast.131), channel_id=1, source_target_pairs={{24,0},{0,8},{8,16},{16,24},{25,1},{1,9},{9,17},{17,25},{26,2},{2,... | collective-permute-start | bytes 4325384 | tf_op jit(solution)/shard_map/ppermute | solution.py:15
  10.3 1.6 collective-permute-start.2
  11.9 1.6 collective-permute-start.3
  13.4 2.2 %collective-permute-start.1 = (bf16[176,2048]{1,0:T(8,128)(2,1)}, bf16[176,2048]{1,0:T(8,128)(2,1)S(1)}, u32[]{:S(2)}, u32[]{:S(2)}) collective-permute-start(bf16[176,2048]{1,0:T(8,128)(2,1)} %bitcast.132), channel_id=1, source_target_pairs={{8,0},{16,8},{24,16},{0,24},{9,1},{17,9},{25,17},{1,25},{10,2},{18... | collective-permute-start | bytes 2162696 | tf_op jit(solution)/shard_map/ppermute | solution.py:15
  16.4 1.2 dynamic_slice.45
  19.8 29.2 %collective-permute-done.2 = bf16[2,44,1024]{2,0,1:T(2,128)(2,1)S(1)} collective-permute-done((bf16[2,44,1024]{2,0,1:T(2,128)(2,1)}, bf16[2,44,1024]{2,0,1:T(2,128)(2,1)S(1)}, u32[]{:S(2)}, u32[]{:S(2)}) %collective-permute-start.2) | collective-permute-done | bytes 180256 | tf_op jit(solution)/shard_map/ppermute | solution.py:15
  49.1 3.6 %collective-permute-done.3 = bf16[2,44,1024]{2,0,1:T(2,128)(2,1)S(1)} collective-permute-done((bf16[2,44,1024]{2,0,1:T(2,128)(2,1)}, bf16[2,44,1024]{2,0,1:T(2,128)(2,1)S(1)}, u32[]{:S(2)}, u32[]{:S(2)}) %collective-permute-start.3) | collective-permute-done | bytes 180256 | tf_op jit(solution)/shard_map/ppermute | solution.py:15
  52.9 12.9 %all-gather = bf16[1,352,1024]{2,0,1:T(2,128)(2,1)S(1)} all-gather(bf16[1,44,1024]{2,0,1:T(2,128)(2,1)S(1)} %constant_dynamic-slice_fusion.3), channel_id=2, replica_groups=mesh['section'=4,'ctx'=2,'tp'=4] {'ctx','tp'}, dimensions={1}, use_global_device_ids=true | all-gather | bytes 811008 | tf_op jit(solution)/shard_map/all_gather | solution.py:43
  65.8 12.0 %all-gather.1 = bf16[1,352,1024]{2,0,1:T(2,128)(2,1)S(1)} all-gather(bf16[1,44,1024]{2,0,1:T(2,128)(2,1)S(1)} %constant_dynamic-slice_fusion.2), channel_id=3, replica_groups=mesh['section'=4,'ctx'=2,'tp'=4] {'ctx','tp'}, dimensions={1}, use_global_device_ids=true | all-gather | bytes 811008 | tf_op jit(solution)/shard_map/all_gather | solution.py:44
  77.8 2.1 %dynamic-slice_reduce_fusion = (bf16[352,256]{1,0:T(8,128)(2,1)S(1)}, bf16[352,256]{1,0:T(8,128)(2,1)S(1)}) fusion(bf16[1,352,1024]{2,0,1:T(2,128)(2,1)S(1)} %all-gather.1, s32[]{:T(128)S(6)} %select_n.30, bf16[1,352,1024]{2,0,1:T(2,128)(2,1)S(1)} %all-gather), kind=kLoop, calls=%fused_computation.47 | loop fusion | bytes 720900 | tf_op jit(solution)/shard_map/dynamic_slice | solution.py:47
  81.1 41.0 %while.36 = (s32[]{:T(128)}, bf16[2,8,176,128]{3,2,1,0:T(8,128)(2,1)}, bf16[2,8,176,128]{3,2,1,0:T(8,128)(2,1)}, f32[2,352,128]{2,1,0:T(8,128)}, f32[2,352,128]{...) while((s32[]{:T(128)}, ...), condition=%wide.region_6.7_spmd.clone, body=%wide.region_0.6_spmd.clone.sunk | while | flops 96633504 | bytes 14739993 | solution.py:90
  83.1 16.4 %while.37 = (s32[]{:T(128)}, f32[352,128]{1,0:T(8,128)S(1)}, f32[352,128]{1,0:T(8,128)S(1)}, bf16[8,176,128]{2,1,0:T(8,128)(2,1)S(1)}, bf16[8,176,128]{2,1,0:T(8...) while((s32[]{:T(128)}, f32[352,128]{1,0:T(8,128)S(1)}, ...), condition=%wide.region_5.5_spmd.clone, body=%wide.region_1.4_spmd.clone.sunk | while | flops 96571552 | bytes 3500700 | solution.py:85
  103.5 16.4 %while.37 = (s32[]{:T(128)}, f32[352,128]{1,0:T(8,128)S(1)}, f32[352,128]{1,0:T(8,128)S(1)}, bf16[8,176,128]{2,1,0:T(8,128)(2,1)S(1)}, bf16[8,176,128]{2,1,0:T(8...) while((s32[]{:T(128)}, f32[352,128]{1,0:T(8,128)S(1)}, ...), condition=%wide.region_5.5_spmd.clone, body=%wide.region_1.4_spmd.clone.sunk | while | flops 96571552 | bytes 3500700 | solution.py:85
  122.2 1.0 copy_bitcast_fusion.2
  123.2 1.0 copy_bitcast_fusion.3
  124.2 1.0 pad_maximum_fusion
  125.2 29.6 %reduce-scatter.2.cloned.1.call-done = f32[176,512]{1,0:T(8,128)} async-done(((f32[352,512]{1,0:T(8,128)}), f32[176,512]{1,0:T(8,128)}) %reduce-scatter.2.cloned.1.call-update) | async-done | bytes 360464 | tf_op jit(solution)/shard_map/reduce_scatter | solution.py:98
  154.8 1.0 fusion.26
  156.5 3.4 %all-to-all-start = ((f32[4,44,256]{2,1,0:T(8,128)}), f32[4,44,256]{2,1,0:T(8,128)S(1)}, u32[]{:S(2)}, u32[]{:S(2)}) async-start(f32[4,44,256]{2,1,0:T(8,128)} %all_to_all.24), calls=%async_computation.1 | async-start | bytes 393216 | tf_op jit(solution)/shard_map/all_to_all | solution.py:102
  160.6 4.6 %all-to-all-done = f32[4,44,256]{2,1,0:T(8,128)S(1)} async-done(((f32[4,44,256]{2,1,0:T(8,128)}), f32[4,44,256]{2,1,0:T(8,128)S(1)}, u32[]{:S(2)}, u32[]{:S(2)}) %all-to-all-start) | async-done | bytes 180256 | tf_op jit(solution)/shard_map/all_to_all | solution.py:102
  165.2 3.4 %all-to-all-start.1 = ((f32[4,44,256]{2,1,0:T(8,128)}), f32[4,44,256]{2,1,0:T(8,128)S(1)}, u32[]{:S(2)}, u32[]{:S(2)}) async-start(f32[4,44,256]{2,1,0:T(8,128)} %all_to_all.27), calls=%async_computation.2 | async-start | bytes 393216 | tf_op jit(solution)/shard_map/all_to_all | solution.py:103
  168.8 1.2 broadcast_in_dim_reshape.7
  170.1 1.2 broadcast_in_dim_reshape.8
  172.3 1.6 all-to-all-done.1
  (211 shorter events, 46.2 us)
Async XLA Ops:
  7.2 147.6 %reduce-scatter.2.cloned.1.call-start = ((), (), s32[]{:S(2)}) async-start(), calls=%async_computation.3 | async-start | bytes 1081344 | tf_op jit(solution)/shard_map/reduce_scatter | solution.py:98
  7.2 73.7 %collective-permute-start = (bf16[2,176,2048]{2,1,0:T(8,128)(2,1)}, bf16[2,176,2048]{2,1,0:T(8,128)(2,1)S(1)}, u32[]{:S(2)}, u32[]{:S(2)}) collective-permute-start(bf16[2,176,2048]{2,1,0:T(8,128)(2,1)} %bitcast.131), channel_id=1, source_target_pairs={{24,0},{0,8},{8,16},{16,24},{25,1},{1,9},{9,17},{17,25},{26,2},{2,... | collective-permute-start | bytes 4325384 | tf_op jit(solution)/shard_map/ppermute | solution.py:15
  10.3 38.7 %collective-permute-start.2 = (bf16[2,44,1024]{2,0,1:T(2,128)(2,1)}, bf16[2,44,1024]{2,0,1:T(2,128)(2,1)S(1)}, u32[]{:S(2)}, u32[]{:S(2)}) collective-permute-start(bf16[2,44,1024]{2,0,1:T(2,128)(2,1)} %bitcast.133), channel_id=1, source_target_pairs={{24,0},{0,8},{8,16},{16,24},{25,1},{1,9},{9,17},{17,25},{26,2},{2,... | collective-permute-start | bytes 540680 | tf_op jit(solution)/shard_map/ppermute | solution.py:15
  11.9 40.8 %collective-permute-start.3 = (bf16[2,44,1024]{2,0,1:T(2,128)(2,1)}, bf16[2,44,1024]{2,0,1:T(2,128)(2,1)S(1)}, u32[]{:S(2)}, u32[]{:S(2)}) collective-permute-start(bf16[2,44,1024]{2,0,1:T(2,128)(2,1)} %bitcast.134), channel_id=1, source_target_pairs={{24,0},{0,8},{8,16},{16,24},{25,1},{1,9},{9,17},{17,25},{26,2},{2,... | collective-permute-start | bytes 540680 | tf_op jit(solution)/shard_map/ppermute | solution.py:15
  13.4 67.3 %collective-permute-start.1 = (bf16[176,2048]{1,0:T(8,128)(2,1)}, bf16[176,2048]{1,0:T(8,128)(2,1)S(1)}, u32[]{:S(2)}, u32[]{:S(2)}) collective-permute-start(bf16[176,2048]{1,0:T(8,128)(2,1)} %bitcast.132), channel_id=1, source_target_pairs={{8,0},{16,8},{24,16},{0,24},{9,1},{17,9},{25,17},{1,25},{10,2},{18... | collective-permute-start | bytes 2162696 | tf_op jit(solution)/shard_map/ppermute | solution.py:15
  81.1 0.9 copy-start
  100.3 1.4 copy-start.1
  101.6 0.9 copy-start
  120.8 1.4 copy-start.1
  125.1 43.4 %copy-start.2 = (bf16[2,8,176,128]{3,2,1,0:T(8,128)(2,1)S(1)}, bf16[2,8,176,128]{3,2,1,0:T(8,128)(2,1)}, u32[]{:S(2)}) copy-start(bf16[2,8,176,128]{3,2,1,0:T(8,128)(2,1)} %get-tuple-element.114) | copy-start | bytes 2162692
  156.5 8.7 %all-to-all-start = ((f32[4,44,256]{2,1,0:T(8,128)}), f32[4,44,256]{2,1,0:T(8,128)S(1)}, u32[]{:S(2)}, u32[]{:S(2)}) async-start(f32[4,44,256]{2,1,0:T(8,128)} %all_to_all.24), calls=%async_computation.1 | async-start | bytes 393216 | tf_op jit(solution)/shard_map/all_to_all | solution.py:102
  165.2 8.7 %all-to-all-start.1 = ((f32[4,44,256]{2,1,0:T(8,128)}), f32[4,44,256]{2,1,0:T(8,128)S(1)}, u32[]{:S(2)}, u32[]{:S(2)}) async-start(f32[4,44,256]{2,1,0:T(8,128)} %all_to_all.27), calls=%async_computation.2 | async-start | bytes 393216 | tf_op jit(solution)/shard_map/all_to_all | solution.py:103
  168.6 1.4 copy-start.3
Sparse Core Ops, SparseCore 0:
  125.3 29.4 reduce-scatter.1
where the time goes:
time: 182 us
  waiting for transfers between devices  68.5 us (38%)
  matrix products  27.9 us (15%)
  blocking collectives  24.9 us (14%)
  local copies, waits for them, and re-layouts  22.2 us (12%)
  between operations  16.1 us (9%)
  starting transfers between devices  15.2 us (8%)
  other arithmetic  5.71 us (3%)
    ppermute x4, waiting for transfers between devices, passed_along(): return lax.ppermute(block, axis, route)  32.7 us
    reduce_scatter x1, waiting for transfers between devices, body(): lax.psum_scatter(grad_terms, 'ctx', scatter_dimension=0, tiled=True)  29.6 us
    all_gather x1, blocking collectives, body(): lax.all_gather(key_rows, ('ctx', 'tp'), axis=0, tiled=True)  12.9 us
    all_gather x1, blocking collectives, body(): lax.all_gather(value_rows, ('ctx', 'tp'), axis=0, tiled=True)  12 us
    ppermute x4, starting transfers between devices, passed_along(): return lax.ppermute(block, axis, route)  8.48 us
    dot_general x16, matrix products, per_head(): jnp.dot(probs_low, value_head, preferred_element_type=jnp.float32)  5.85 us
    dot_general x16, matrix products, per_head(): jnp.dot(probs_low.T, do_one, preferred_element_type=jnp.float32)  5.85 us
    dot_general x16, matrix products, per_head(): jnp.dot(q_one, key_head.T, preferred_element_type=jnp.float32) * scale  4.9 us
  transfers between devices with their start and end apart: 7, of which 5 were waited for; matrix products, arithmetic and copies ran while one was open for 5% of the time, Pallas kernels for 0%

commit v1 on v0

v1 whole, which is shorter than its diff:
```python
import functools
import math

import jax
import jax.numpy as jnp
from jax import lax
from jax.experimental import pallas as pl
from jax.experimental.pallas import tpu as pltpu
from jax.sharding import PartitionSpec as P

HEAD_DIM = 128
NEG = -1e30
MESH = pl.DeviceIdType.MESH
F32 = jnp.float32
BF16 = jnp.bfloat16


def nt_dot(a, b):
    return lax.dot_general(a, b, (((1,), (1,)), ((), ())), preferred_element_type=F32)


def tn_dot(a, b):
    return lax.dot_general(a, b, (((0,), (0,)), ((), ())), preferred_element_type=F32)


def kernel(
    dims,
    order_ref, plan_ref, q_hbm, k_hbm, v_hbm, do_hbm,
    attn_hbm, dq_hbm, dk_hbm, dv_hbm,
    q_in, q_send, q_got, do_got, k_in, v_in, kv_send, kv_all, bias,
    attn_buf, dq_buf, dk_acc, dv_acc, g_send, g_got, dk_out, dv_out,
    q_lsem, k_lsem, q_ssem, q_rsem, do_ssem, do_rsem, kv_ssem, kv_rsem, fw_ssem,
    g_ssem, g_rsem, out_sem, grad_sem,
):
    S, C, TP, R, KR, KP, kl, group, CH, block_len = dims
    hd = HEAD_DIM
    W = kl * hd
    NB = C * TP
    KK = NB * KP
    CW = CH * hd
    per_kv = group // CH
    chunks = kl * per_kv
    slots = NB * KR // block_len
    s, c, t = lax.axis_index("section"), lax.axis_index("ctx"), lax.axis_index("tp")
    me = c * TP + t
    after, before = lax.rem(s + 1, S), lax.rem(s + S - 1, S)

    def q_load(i):
        cols = pl.ds(pl.multiple_of(i * CW, CW), CW)
        return pltpu.make_async_copy(q_hbm.at[0, :, :, cols], q_in.at[i], q_lsem.at[i])

    k_load = pltpu.make_async_copy(k_hbm.at[0], k_in, k_lsem.at[0])
    v_load = pltpu.make_async_copy(v_hbm.at[0], v_in, k_lsem.at[1])
    k_load.start()
    v_load.start()
    for i in range(chunks):
        q_load(i).start()

    barrier = pltpu.get_barrier_semaphore()

    @pl.loop(0, TP)
    def _(u):
        pl.semaphore_signal(barrier, inc=1, device_id={"section": after, "ctx": c, "tp": u}, device_id_type=MESH)
        pl.semaphore_signal(barrier, inc=1, device_id={"section": before, "ctx": c, "tp": u}, device_id_type=MESH)

    @pl.loop(1, NB)
    def _(o):
        b = lax.rem(me + o, NB)
        pl.semaphore_signal(barrier, inc=1, device_id={"section": s, "ctx": b // TP, "tp": lax.rem(b, TP)}, device_id_type=MESH)

    def do_copy(i):
        cols = pl.ds(pl.multiple_of(i * CW, CW), CW)
        return pltpu.make_async_remote_copy(
            src_ref=do_hbm.at[0, :, cols], dst_ref=do_got.at[i],
            send_sem=do_ssem.at[i], recv_sem=do_rsem.at[i],
            device_id={"section": before, "ctx": c, "tp": t}, device_id_type=MESH)

    def q_copy(i):
        return pltpu.make_async_remote_copy(
            src_ref=q_send.at[i], dst_ref=q_got.at[i],
            send_sem=q_ssem.at[i], recv_sem=q_rsem.at[i],
            device_id={"section": after, "ctx": c, "tp": t}, device_id_type=MESH)

    def kv_copy(u, b):
        return pltpu.make_async_remote_copy(
            src_ref=kv_send.at[u], dst_ref=kv_all.at[b],
            send_sem=kv_ssem.at[u], recv_sem=kv_rsem.at[b],
            device_id={"section": after, "ctx": c, "tp": u}, device_id_type=MESH)

    def kv_forward(b, u, to):
        return pltpu.make_async_remote_copy(
            src_ref=kv_all.at[b], dst_ref=kv_all.at[b],
            send_sem=fw_ssem.at[u, to], recv_sem=kv_rsem.at[b],
            device_id={"section": s, "ctx": to, "tp": t}, device_id_type=MESH)

    def g_copy(g, to, frm):
        return pltpu.make_async_remote_copy(
            src_ref=g_send.at[g, to], dst_ref=g_got.at[g, frm],
            send_sem=g_ssem.at[g, to], recv_sem=g_rsem.at[g, frm],
            device_id={"section": s, "ctx": to // TP, "tp": lax.rem(to, TP)}, device_id_type=MESH)

    slot = plan_ref[after]

    def picked(options):
        value = options[0]
        for m in range(1, len(options)):
            value = jnp.where(slot == m, options[m], value)
        return value

    k_load.wait()
    v_load.wait()
    for u in range(TP):
        for kind, src in enumerate((k_in, v_in)):
            if KP != KR:
                kv_send[u, kind, KP - 16:, :] = jnp.zeros((16, W), BF16)
            kv_send[u, kind, :KR, :] = picked(
                [src[m, :, u * W:(u + 1) * W] for m in range(src.shape[0])])

    pl.semaphore_wait(barrier, 2 * TP + NB - 1)

    for o in range(TP):
        u = lax.rem(t + o, TP)
        kv_copy(u, me).start()
    for i in range(chunks):
        q_load(i).wait()
        q_send[i] = picked([q_in[i, m] for m in range(q_in.shape[1])])
        q_copy(i).start()
        do_copy(i).start()

    col = lax.broadcasted_iota(jnp.int32, (1, KK), 1)
    blk = col // KP
    inner = col - blk * KP
    store_row = blk * KR + inner
    key_slot = store_row // block_len
    key_pos = store_row - key_slot * block_len
    for j in range(slots):
        key_pos = key_pos + jnp.where(key_slot == j, order_ref[j] * block_len, 0)
    key_pos = jnp.where(inner < KR, key_pos, jnp.int32(2**30))
    row = lax.broadcasted_iota(jnp.int32, (R, 1), 0)
    query_pos = row
    for j in range(R // block_len):
        base = order_ref[c * (R // block_len) + j] * block_len - j * block_len
        query_pos = query_pos + jnp.where(row // block_len == j, base, 0)
    bias[...] = jnp.where(key_pos <= query_pos, 0.0, NEG).astype(F32)

    for o in range(TP):
        u = lax.rem(t + TP - o, TP)
        b = c * TP + u
        kv_copy(t, b).wait_recv()

        @pl.loop(1, C)
        def _(k):
            kv_forward(b, u, lax.rem(c + k, C)).start()

    @pl.loop(TP, NB)
    def _(o):
        b = lax.rem(c * TP + o, NB)
        kv_copy(t, b).wait_recv()

    scale = hd ** -0.5
    scale2 = scale * math.log2(math.e)

    def out_copies(i):
        cols = pl.ds(pl.multiple_of(i * CW, CW), CW)
        return (
            pltpu.make_async_copy(attn_buf.at[i], attn_hbm.at[0, :, cols], out_sem.at[0, i]),
            pltpu.make_async_copy(dq_buf.at[i], dq_hbm.at[0, :, cols], out_sem.at[1, i]),
        )

    for g in range(kl):
        gc = slice(g * hd, (g + 1) * hd)
        dk_acc[...] = jnp.zeros_like(dk_acc)
        dv_acc[...] = jnp.zeros_like(dv_acc)

        @pl.loop(0, per_kv)
        def _(n):
            i = g * per_kv + n
            keys = kv_all[:, 0, :, gc].reshape(KK, hd)
            values = kv_all[:, 1, :, gc].reshape(KK, hd)
            q_copy(i).wait_recv()
            do_copy(i).wait_recv()
            for h in range(CH):
                hc = slice(h * hd, (h + 1) * hd)
                q = q_got[i, :, hc]
                do = do_got[i, :, hc]
                scores = nt_dot(q, keys) * scale2 + bias[...]
                top = jnp.max(scores, axis=1, keepdims=True)
                e = jnp.exp2(scores - top)
                total = jnp.sum(e, axis=1, keepdims=True)
                probs = e * (1.0 / total)
                low = probs.astype(BF16)
                attended = jnp.dot(low, values, preferred_element_type=F32)
                delta = jnp.sum(do.astype(F32) * attended, axis=1, keepdims=True)
                dprobs = nt_dot(do, values)
                ds = (probs * (dprobs - delta)).astype(BF16)
                attn_buf[i, :, hc] = attended.astype(BF16)
                dq_buf[i, :, hc] = (jnp.dot(ds, keys, preferred_element_type=F32) * scale).astype(BF16)
                dk_acc[...] += tn_dot(q, ds)
                dv_acc[...] += tn_dot(do, low)
            for copy in out_copies(i):
                copy.start()

        g_send[g, :, 0] = (dk_acc[...] * scale).T.astype(BF16).reshape(NB, KP, hd)
        g_send[g, :, 1] = dv_acc[...].T.astype(BF16).reshape(NB, KP, hd)

        @pl.loop(1, NB)
        def _(o):
            g_copy(g, lax.rem(me + o, NB), me).start()

        g_got[g, me] = g_send[g, me]

    for g in range(kl):
        @pl.loop(1, NB)
        def _(o):
            g_copy(g, me, lax.rem(me + o, NB)).wait_recv()

        for u in range(TP):
            cols = slice((u * kl + g) * hd, (u * kl + g + 1) * hd)
            for kind, out in enumerate((dk_out, dv_out)):
                total = g_got[g, u, kind].astype(F32)
                for cc in range(1, C):
                    total = total + g_got[g, cc * TP + u, kind].astype(F32)
                out[:, cols] = total[:KR]
    dk_copy = pltpu.make_async_copy(dk_out, dk_hbm.at[0], grad_sem.at[0])
    dv_copy = pltpu.make_async_copy(dv_out, dv_hbm.at[0], grad_sem.at[1])
    dk_copy.start()
    dv_copy.start()

    @pl.loop(0, TP)
    def _(u):
        kv_copy(u, me).wait_send()

        @pl.loop(1, C)
        def _(k):
            kv_forward(c * TP + u, u, lax.rem(c + k, C)).wait_send()

    for g in range(kl):
        @pl.loop(1, NB)
        def _(o):
            g_copy(g, lax.rem(me + o, NB), me).wait_send()

    for i in range(chunks):
        q_copy(i).wait_send()
        do_copy(i).wait_send()
        for copy in out_copies(i):
            copy.wait()
    dk_copy.wait()
    dv_copy.wait()


def solution(mesh):
    S, C, TP = mesh.shape["section"], mesh.shape["ctx"], mesh.shape["tp"]

    def body(block_order, plan, q_box, k_box, v_box, grad_out):
        hd = HEAD_DIM
        R, QC = q_box.shape[2:]
        KR, KW = k_box.shape[2:]
        block_len = R * C // block_order.shape[0]
        kl = KW // hd // TP
        group = QC // hd // kl
        CH = 2
        KP = -(-KR // 16) * 16
        NB = C * TP
        W = kl * hd
        CW = CH * hd
        chunks = QC // CW
        dims = (S, C, TP, R, KR, KP, kl, group, CH, block_len)
        dma = pltpu.SemaphoreType.DMA
        anywhere = pl.BlockSpec(memory_space=pl.ANY)
        smem = pl.BlockSpec(memory_space=pltpu.SMEM)
        return pl.pallas_call(
            functools.partial(kernel, dims),
            out_shape=(
                jax.ShapeDtypeStruct((1, R, QC), BF16),
                jax.ShapeDtypeStruct((1, R, QC), BF16),
                jax.ShapeDtypeStruct((1, KR, KW), F32),
                jax.ShapeDtypeStruct((1, KR, KW), F32),
            ),
            in_specs=[smem, smem] + [anywhere] * 4,
            out_specs=[anywhere] * 4,
            scratch_shapes=[
                pltpu.VMEM((chunks, q_box.shape[1], R, CW), BF16),
                pltpu.VMEM((chunks, R, CW), BF16),
                pltpu.VMEM((chunks, R, CW), BF16),
                pltpu.VMEM((chunks, R, CW), BF16),
                pltpu.VMEM(k_box.shape[1:], BF16),
                pltpu.VMEM(k_box.shape[1:], BF16),
                pltpu.VMEM((TP, 2, KP, W), BF16),
                pltpu.VMEM((NB, 2, KP, W), BF16),
                pltpu.VMEM((R, NB * KP), F32),
                pltpu.VMEM((chunks, R, CW), BF16),
                pltpu.VMEM((chunks, R, CW), BF16),
                pltpu.VMEM((hd, NB * KP), F32),
                pltpu.VMEM((hd, NB * KP), F32),
                pltpu.VMEM((kl, NB, 2, KP, hd), BF16),
                pltpu.VMEM((kl, NB, 2, KP, hd), BF16),
                pltpu.VMEM((KR, KW), F32),
                pltpu.VMEM((KR, KW), F32),
                dma((chunks,)), dma((2,)), dma((chunks,)), dma((chunks,)), dma((chunks,)), dma((chunks,)),
                dma((TP,)), dma((NB,)), dma((TP, C)), dma((kl, NB)), dma((kl, NB)), dma((2, chunks)), dma((2,)),
            ],
            compiler_params=pltpu.CompilerParams(
                collective_id=0, has_side_effects=True, vmem_limit_bytes=40 * 1024 * 1024
            ),
        )(block_order, plan, q_box, k_box, v_box, grad_out)

    in_specs = (
        P(),
        P(),
        P("section", None, "ctx", "tp"),
        P("section", None, ("ctx", "tp"), None),
        P("section", None, ("ctx", "tp"), None),
        P("section", "ctx", "tp"),
    )
    out_specs = (
        P("section", "ctx", "tp"),
        P("section", "ctx", "tp"),
        P("section", ("ctx", "tp"), None),
        P("section", ("ctx", "tp"), None),
    )
    return jax.shard_map(body, mesh=mesh, in_specs=in_specs, out_specs=out_specs, check_vma=False)
```

time: 182 us -> 60.4 us (0.33)
  waiting for transfers between devices: 68.5 us -> 0 us
  Pallas kernels: 0 us -> 50.4 us
  matrix products: 27.9 us -> 0 us
  blocking collectives: 24.9 us -> 0 us
  between operations: 16.1 us -> 0.66 us
  starting transfers between devices: 15.2 us -> 0 us
  local copies, waits for them, and re-layouts: 22.2 us -> 9.12 us
  other arithmetic: 5.71 us -> 0 us
    pallas_call x0 -> x1, Pallas kernels: none -> 50.4 us  [body(): pl.pallas_call(functools.partial(kernel, dims), out_shape=(jax.ShapeDtype...]
    ppermute x4 -> x0, waiting for transfers between devices: 32.7 us -> none  [passed_along(): return lax.ppermute(block, axis, route)]
    reduce_scatter x1 -> x0, waiting for transfers between devices: 29.6 us -> none  [body(): lax.psum_scatter(grad_terms, 'ctx', scatter_dimension=0, tiled=True)]
    dot_general x96 -> x0, matrix products: 27.9 us -> none  [the longest x16 5.85 us: per_head(): jnp.dot(probs_low, value_head, preferred_element_type=jnp.float32)]
    all_gather x2 -> x0, blocking collectives: 24.9 us -> none  [the longest x1 12.9 us: body(): lax.all_gather(key_rows, ('ctx', 'tp'), axis=0, tiled=True)]
    ppermute x4 -> x0, starting transfers between devices: 8.48 us -> none  [passed_along(): return lax.ppermute(block, axis, route)]
    all_to_all x2 -> x0, starting transfers between devices: 6.73 us -> none  [the longest x1 3.37 us: body(): lax.all_to_all(key_part, 'tp', split_axis=0, concat_axis=1, tiled=True)]
    unnamed x9 -> x12, local copies, waits for them, and re-layouts: 1.1 us -> 7.4 us
  transfers between devices with their start and end apart: 7 -> 0, of which waited for: 5 -> 0; matrix products, arithmetic and copies ran while one was open for 5% -> 0% of each run, Pallas kernels for 0% -> 0%
where the time goes in v1:
time: 60.4 us; the launch traced here: 60.2 us
  Pallas kernels  50.4 us (83%)
  local copies, waits for them, and re-layouts  9.12 us (15%)
  between operations  0.66 us (1%)
    pallas_call x1, Pallas kernels, body(): pl.pallas_call(functools.partial(kernel, dims), out_shape=(jax.ShapeDtype...  50.4 us
    unnamed x12, local copies, waits for them, and re-layouts  7.4 us
    pallas_call x2, local copies, waits for them, and re-layouts, body(): pl.pallas_call(functools.partial(kernel, dims), out_shape=(jax.ShapeDtype...  1.71 us

profile of v1, /device:TPU:0, one launch (start us, length us, event | category | flops | bytes accessed | tf_op | source)
XLA Modules:
  0.0 60.2 jit_solution(9389573572658221961)
XLA Ops:
  0.6 1.0 %copy.10.k_hbm = bf16[1,2,44,1024]{3,2,1,0:T(8,128)(2,1)S(1)} copy(bf16[1,2,44,1024]{3,1,2,0:T(2,128)(2,1)} %param.9) | data formatting | bytes 360448 | tf_op args[3]
  1.6 1.0 %copy.11.v_hbm = bf16[1,2,44,1024]{3,2,1,0:T(8,128)(2,1)S(1)} copy(bf16[1,2,44,1024]{3,1,2,0:T(2,128)(2,1)} %param.10) | data formatting | bytes 360448 | tf_op args[4]
  2.6 0.0 copy-start
  2.6 1.4 %copy-done = bf16[1,2,176,2048]{3,2,1,0:T(8,128)(2,1)S(1)} copy-done((bf16[1,2,176,2048]{3,2,1,0:T(8,128)(2,1)S(1)}, bf16[1,2,176,2048]{3,2,1,0:T(8,128)(2,1)}, u32[]{:S(2)}) %copy-start) | copy-done | bytes 1441816
  3.9 0.0 copy-start.1
  3.9 1.1 %copy-done.1 = bf16[1,176,2048]{2,1,0:T(8,128)(2,1)S(1)} copy-done((bf16[1,176,2048]{2,1,0:T(8,128)(2,1)S(1)}, bf16[1,176,2048]{2,1,0:T(8,128)(2,1)}, u32[]{:S(2)}) %copy-start.1) | copy-done | bytes 720920
  5.0 0.0 copy-start.2
  5.0 0.7 %copy-done.2 = s32[4]{0:T(128)S(1)} copy-done((s32[4]{0:T(128)S(1)}, s32[4]{0:T(128)}, u32[]{:S(2)}) %copy-start.2) | copy-done | bytes 40
  5.7 0.0 copy-start.3
  5.7 0.7 %copy-done.3 = s32[4]{0:T(128)S(1)} copy-done((s32[4]{0:T(128)S(1)}, s32[4]{0:T(128)}, u32[]{:S(2)}) %copy-start.3) | copy-done | bytes 40
  6.3 50.4 %shard_map.93 = (bf16[1,176,2048]{2,1,0:T(8,128)(2,1)S(1)}, bf16[1,176,2048]{2,1,0:T(8,128)(2,1)S(1)}, f32[1,44,1024]{2,1,0:T(8,128)S(1)}, f32[1,44,1024]{2,1,0:T(8,128)S(1)}) custom-call(s32[4]{0:T(128)S(1)} %copy-done.2, s32[4]{0:T(128)S(1)} %copy-done.3, bf16[1,2,176,2048]{3,2,1,0:T(8,128)(2,1)S(1)} %copy-done, bf16[1,2,44,1024]{3,2,1,0:T(8,128)(2,1)S(1)} %copy.10.k_hbm, ...), custom_call_target="tpu_custom_call" | custom-call | tf_op jit(solution)/shard_map/pallas_call | solution.py:271
  56.7 0.9 %copy.12 = f32[1,44,1024]{2,0,1:T(1,128)} copy(f32[1,44,1024]{2,1,0:T(8,128)S(1)} %get-tuple-element.6) | data formatting | bytes 360448 | tf_op jit(solution)/shard_map/pallas_call | solution.py:271
  57.6 0.9 %copy.13 = f32[1,44,1024]{2,0,1:T(1,128)} copy(f32[1,44,1024]{2,1,0:T(8,128)S(1)} %get-tuple-element.7) | data formatting | bytes 360448 | tf_op jit(solution)/shard_map/pallas_call | solution.py:271
  58.4 0.9 %copy.16 = bf16[1,176,2048]{2,1,0:T(8,128)(2,1)} copy(bf16[1,176,2048]{2,1,0:T(8,128)(2,1)S(1)} %get-tuple-element.12) | data formatting | bytes 1441792
  59.3 0.9 %copy.17 = bf16[1,176,2048]{2,1,0:T(8,128)(2,1)} copy(bf16[1,176,2048]{2,1,0:T(8,128)(2,1)S(1)} %get-tuple-element.13) | data formatting | bytes 1441792
Async XLA Ops:
  2.6 1.4 %copy-start = (bf16[1,2,176,2048]{3,2,1,0:T(8,128)(2,1)S(1)}, bf16[1,2,176,2048]{3,2,1,0:T(8,128)(2,1)}, u32[]{:S(2)}) copy-start(bf16[1,2,176,2048]{3,2,1,0:T(8,128)(2,1)} %q_hbm.1) | copy-start | bytes 4325380
  3.9 1.1 %copy-start.1 = (bf16[1,176,2048]{2,1,0:T(8,128)(2,1)S(1)}, bf16[1,176,2048]{2,1,0:T(8,128)(2,1)}, u32[]{:S(2)}) copy-start(bf16[1,176,2048]{2,1,0:T(8,128)(2,1)} %do_hbm.1) | copy-start | bytes 2162692
  5.0 0.7 %copy-start.2 = (s32[4]{0:T(128)S(1)}, s32[4]{0:T(128)}, u32[]{:S(2)}) copy-start(s32[4]{0:T(128)} %order_ref.1) | copy-start | bytes 52
  5.7 0.7 %copy-start.3 = (s32[4]{0:T(128)S(1)}, s32[4]{0:T(128)}, u32[]{:S(2)}) copy-start(s32[4]{0:T(128)} %plan_ref.1) | copy-start | bytes 52

commit v2 on v1

--- a/solution.py
+++ b/solution.py
@@ -25,9 +25,9 @@
 
 def kernel(
     dims,
-    order_ref, plan_ref, q_hbm, k_hbm, v_hbm, do_hbm,
+    order_hbm, plan_hbm, q_hbm, k_hbm, v_hbm, do_hbm,
     attn_hbm, dq_hbm, dk_hbm, dv_hbm,
-    q_in, q_send, q_got, do_got, k_in, v_in, kv_send, kv_all, bias,
+    order_ref, plan_ref, q_in, q_send, q_got, do_got, k_in, v_in, kv_send, kv_all, bias,
     attn_buf, dq_buf, dk_acc, dv_acc, g_send, g_got, dk_out, dv_out,
     q_lsem, k_lsem, q_ssem, q_rsem, do_ssem, do_rsem, kv_ssem, kv_rsem, fw_ssem,
     g_ssem, g_rsem, out_sem, grad_sem,
@@ -51,6 +51,10 @@
 
     k_load = pltpu.make_async_copy(k_hbm.at[0], k_in, k_lsem.at[0])
     v_load = pltpu.make_async_copy(v_hbm.at[0], v_in, k_lsem.at[1])
+    order_load = pltpu.make_async_copy(order_hbm, order_ref, k_lsem.at[2])
+    plan_load = pltpu.make_async_copy(plan_hbm, plan_ref, k_lsem.at[3])
+    plan_load.start()
+    order_load.start()
     k_load.start()
     v_load.start()
     for i in range(chunks):
@@ -99,6 +103,7 @@
             send_sem=g_ssem.at[g, to], recv_sem=g_rsem.at[g, frm],
             device_id={"section": s, "ctx": to // TP, "tp": lax.rem(to, TP)}, device_id_type=MESH)
 
+    plan_load.wait()
     slot = plan_ref[after]
 
     def picked(options):
@@ -107,25 +112,32 @@
             value = jnp.where(slot == m, options[m], value)
         return value
 
+    def send_chunk(i):
+        do_copy(i).start()
+        q_load(i).wait()
+        q_send[i] = picked([q_in[i, m] for m in range(q_in.shape[1])])
+        q_copy(i).start()
+
+    pl.semaphore_wait(barrier, 2 * TP + NB - 1)
+    first = min(2, chunks)
+    for i in range(first):
+        send_chunk(i)
+
     k_load.wait()
     v_load.wait()
-    for u in range(TP):
-        for kind, src in enumerate((k_in, v_in)):
+    for kind, src in enumerate((k_in, v_in)):
+        rows = picked([src[:, m, :] for m in range(src.shape[1])])
+        for u in range(TP):
             if KP != KR:
                 kv_send[u, kind, KP - 16:, :] = jnp.zeros((16, W), BF16)
-            kv_send[u, kind, :KR, :] = picked(
-                [src[m, :, u * W:(u + 1) * W] for m in range(src.shape[0])])
-
-    pl.semaphore_wait(barrier, 2 * TP + NB - 1)
-
+            kv_send[u, kind, :KR, :] = rows[:, u * W:(u + 1) * W]
     for o in range(TP):
         u = lax.rem(t + o, TP)
         kv_copy(u, me).start()
-    for i in range(chunks):
-        q_load(i).wait()
-        q_send[i] = picked([q_in[i, m] for m in range(q_in.shape[1])])
-        q_copy(i).start()
-        do_copy(i).start()
+    for i in range(first, chunks):
+        send_chunk(i)
+
+    order_load.wait()
 
     col = lax.broadcasted_iota(jnp.int32, (1, KK), 1)
     blk = col // KP
@@ -220,9 +232,9 @@
                 total = g_got[g, u, kind].astype(F32)
                 for cc in range(1, C):
                     total = total + g_got[g, cc * TP + u, kind].astype(F32)
-                out[:, cols] = total[:KR]
-    dk_copy = pltpu.make_async_copy(dk_out, dk_hbm.at[0], grad_sem.at[0])
-    dv_copy = pltpu.make_async_copy(dv_out, dv_hbm.at[0], grad_sem.at[1])
+                out[:, 0, cols] = total[:KR]
+    dk_copy = pltpu.make_async_copy(dk_out, dk_hbm, grad_sem.at[0])
+    dv_copy = pltpu.make_async_copy(dv_out, dv_hbm, grad_sem.at[1])
     dk_copy.start()
     dv_copy.start()
 
@@ -246,6 +258,15 @@
             copy.wait()
     dk_copy.wait()
     dv_copy.wait()
+
+
+def write_out(*refs):
+    sems = refs[-1]
+    copies = [pltpu.make_async_copy(refs[j], refs[4 + j], sems.at[j]) for j in range(4)]
+    for copy in copies:
+        copy.start()
+    for copy in copies:
+        copy.wait()
 
 
 def solution(mesh):
@@ -267,24 +288,26 @@
         dims = (S, C, TP, R, KR, KP, kl, group, CH, block_len)
         dma = pltpu.SemaphoreType.DMA
         anywhere = pl.BlockSpec(memory_space=pl.ANY)
-        smem = pl.BlockSpec(memory_space=pltpu.SMEM)
-        return pl.pallas_call(
+        hbm = pl.BlockSpec(memory_space=pltpu.HBM)
+        results = pl.pallas_call(
             functools.partial(kernel, dims),
             out_shape=(
-                jax.ShapeDtypeStruct((1, R, QC), BF16),
-                jax.ShapeDtypeStruct((1, R, QC), BF16),
-                jax.ShapeDtypeStruct((1, KR, KW), F32),
-                jax.ShapeDtypeStruct((1, KR, KW), F32),
+                pltpu.VMEM((1, R, QC), BF16),
+                pltpu.VMEM((1, R, QC), BF16),
+                pltpu.VMEM((KR, 1, KW), F32),
+                pltpu.VMEM((KR, 1, KW), F32),
             ),
-            in_specs=[smem, smem] + [anywhere] * 4,
+            in_specs=[hbm] * 6,
             out_specs=[anywhere] * 4,
             scratch_shapes=[
+                pltpu.SMEM(block_order.shape, jnp.int32),
+                pltpu.SMEM(plan.shape, jnp.int32),
                 pltpu.VMEM((chunks, q_box.shape[1], R, CW), BF16),
                 pltpu.VMEM((chunks, R, CW), BF16),
                 pltpu.VMEM((chunks, R, CW), BF16),
                 pltpu.VMEM((chunks, R, CW), BF16),
-                pltpu.VMEM(k_box.shape[1:], BF16),
-                pltpu.VMEM(k_box.shape[1:], BF16),
+                pltpu.VMEM((KR, k_box.shape[1], KW), BF16),
+                pltpu.VMEM((KR, k_box.shape[1], KW), BF16),
                 pltpu.VMEM((TP, 2, KP, W), BF16),
                 pltpu.VMEM((NB, 2, KP, W), BF16),
                 pltpu.VMEM((R, NB * KP), F32),
@@ -294,15 +317,24 @@
                 pltpu.VMEM((hd, NB * KP), F32),
                 pltpu.VMEM((kl, NB, 2, KP, hd), BF16),
                 pltpu.VMEM((kl, NB, 2, KP, hd), BF16),
-                pltpu.VMEM((KR, KW), F32),
-                pltpu.VMEM((KR, KW), F32),
-                dma((chunks,)), dma((2,)), dma((chunks,)), dma((chunks,)), dma((chunks,)), dma((chunks,)),
+                pltpu.VMEM((KR, 1, KW), F32),
+                pltpu.VMEM((KR, 1, KW), F32),
+                dma((chunks,)), dma((4,)), dma((chunks,)), dma((chunks,)), dma((chunks,)), dma((chunks,)),
                 dma((TP,)), dma((NB,)), dma((TP, C)), dma((kl, NB)), dma((kl, NB)), dma((2, chunks)), dma((2,)),
             ],
             compiler_params=pltpu.CompilerParams(
-                collective_id=0, has_side_effects=True, vmem_limit_bytes=40 * 1024 * 1024
+                collective_id=0, has_side_effects=True, vmem_limit_bytes=56 * 1024 * 1024
             ),
-        )(block_order, plan, q_box, k_box, v_box, grad_out)
+        )(block_order, plan, q_box, k_box.transpose(0, 2, 1, 3), v_box.transpose(0, 2, 1, 3), grad_out)
+        attn, dq, dk, dv = pl.pallas_call(
+            write_out,
+            out_shape=tuple(jax.ShapeDtypeStruct(r.shape, r.dtype) for r in results),
+            in_specs=[anywhere] * 4,
+            out_specs=[hbm] * 4,
+            scratch_shapes=[dma((4,))],
+            compiler_params=pltpu.CompilerParams(vmem_limit_bytes=8 * 1024 * 1024),
+        )(*results)
+        return attn, dq, dk.transpose(1, 0, 2), dv.transpose(1, 0, 2)
 
     in_specs = (
         P(),

time: 60.4 us -> 52.6 us (0.87)
  local copies, waits for them, and re-layouts: 9.12 us -> 0 us
  Pallas kernels: 50.4 us -> 51.8 us
    unnamed x12 -> x0, local copies, waits for them, and re-layouts: 7.4 us -> none
    pallas_call x2 -> x0, local copies, waits for them, and re-layouts: 1.71 us -> none  [body(): pl.pallas_call(functools.partial(kernel, dims), out_shape=(jax.ShapeDtype...]
    pallas_call x1 -> x2, Pallas kernels: 50.4 us -> 51.8 us  [the longest x1 50.5 us: body(): pl.pallas_call(functools.partial(kernel, dims), out_shape=(pltpu.VMEM((1,...]
where the time goes in v2:
time: 52.6 us; the launch traced here: 52.4 us
  Pallas kernels  51.8 us (98%)
  between operations  0.64 us (1%)
    pallas_call x1, Pallas kernels, body(): pl.pallas_call(functools.partial(kernel, dims), out_shape=(pltpu.VMEM((1,...  50.5 us
    pallas_call x1, Pallas kernels, body(): pl.pallas_call(write_out, out_shape=tuple((jax.ShapeDtypeStruct(r.shape,...  1.24 us

profile of v2, /device:TPU:0, one launch (start us, length us, event | category | flops | bytes accessed | tf_op | source)
XLA Modules:
  0.0 52.4 jit_solution(2027150493421531458)
XLA Ops:
  0.6 50.5 %shard_map.93 = (bf16[1,176,2048]{2,1,0:T(8,128)(2,1)S(1)}, bf16[1,176,2048]{2,1,0:T(8,128)(2,1)S(1)}, f32[44,1,1024]{2,1,0:T(1,128)S(1)}, f32[44,1,1024]{2,1,0:T(1,128)S(1)}) custom-call(s32[4]{0:T(128)} %order_hbm.1, s32[4]{0:T(128)} %plan_hbm.1, bf16[1,2,176,2048]{3,2,1,0:T(8,128)(2,1)} %q_hbm.1, bf16[1,44,2,1024]{3,2,1,0:T(2,128)(2,1)} %bitcast.4, ...), custom_call_target="tpu_custom_call" | custom-call | tf_op jit(solution)/shard_map/pallas_call | solution.py:292
  51.2 1.2 %shard_map.94 = (bf16[1,176,2048]{2,1,0:T(8,128)(2,1)}, bf16[1,176,2048]{2,1,0:T(8,128)(2,1)}, f32[44,1,1024]{2,1,0:T(1,128)}, f32[44,1,1024]{2,1,0:T(1,128)}) custom-call(bf16[1,176,2048]{2,1,0:T(8,128)(2,1)S(1)} %get-tuple-element.12.refs_0_, bf16[1,176,2048]{2,1,0:T(8,128)(2,1)S(1)} %get-tuple-element.13.refs_1_, ...), custom_call_target="tpu_custom_call" | custom-call | tf_op jit(solution)/shard_map/pallas_call | solution.py:329

commit v3 on v2

--- a/solution.py
+++ b/solution.py
@@ -119,7 +119,7 @@
         q_copy(i).start()
 
     pl.semaphore_wait(barrier, 2 * TP + NB - 1)
-    first = min(2, chunks)
+    first = min(4, chunks)
     for i in range(first):
         send_chunk(i)
 
@@ -212,8 +212,8 @@
             for copy in out_copies(i):
                 copy.start()
 
-        g_send[g, :, 0] = (dk_acc[...] * scale).T.astype(BF16).reshape(NB, KP, hd)
-        g_send[g, :, 1] = dv_acc[...].T.astype(BF16).reshape(NB, KP, hd)
+        g_send[g, :, 0] = (dk_acc[...] * scale).astype(BF16).T.reshape(NB, KP, hd)
+        g_send[g, :, 1] = dv_acc[...].astype(BF16).T.reshape(NB, KP, hd)
 
         @pl.loop(1, NB)
         def _(o):
@@ -279,7 +279,7 @@
         block_len = R * C // block_order.shape[0]
         kl = KW // hd // TP
         group = QC // hd // kl
-        CH = 2
+        CH = 1
         KP = -(-KR // 16) * 16
         NB = C * TP
         W = kl * hd

time: 52.6 us -> 52.4 us (level)
  no operation moved by 1% of the time
where the time goes in v3:
time: 52.4 us; the launch traced here: 52.2 us
  Pallas kernels  51.6 us (98%)
  between operations  0.64 us (1%)
    pallas_call x1, Pallas kernels, body(): pl.pallas_call(functools.partial(kernel, dims), out_shape=(pltpu.VMEM((1,...  50.4 us
    pallas_call x1, Pallas kernels, body(): pl.pallas_call(write_out, out_shape=tuple((jax.ShapeDtypeStruct(r.shape,...  1.24 us

profile of v3, /device:TPU:0, one launch (start us, length us, event | category | flops | bytes accessed | tf_op | source)
XLA Modules:
  0.0 52.2 jit_solution(12831903032103336348)
XLA Ops:
  0.6 50.4 %shard_map.93 = (bf16[1,176,2048]{2,1,0:T(8,128)(2,1)S(1)}, bf16[1,176,2048]{2,1,0:T(8,128)(2,1)S(1)}, f32[44,1,1024]{2,1,0:T(1,128)S(1)}, f32[44,1,1024]{2,1,0:T(1,128)S(1)}) custom-call(s32[4]{0:T(128)} %order_hbm.1, s32[4]{0:T(128)} %plan_hbm.1, bf16[1,2,176,2048]{3,2,1,0:T(8,128)(2,1)} %q_hbm.1, bf16[1,44,2,1024]{3,2,1,0:T(2,128)(2,1)} %bitcast.4, ...), custom_call_target="tpu_custom_call" | custom-call | tf_op jit(solution)/shard_map/pallas_call | solution.py:292
  51.0 1.2 %shard_map.94 = (bf16[1,176,2048]{2,1,0:T(8,128)(2,1)}, bf16[1,176,2048]{2,1,0:T(8,128)(2,1)}, f32[44,1,1024]{2,1,0:T(1,128)}, f32[44,1,1024]{2,1,0:T(1,128)}) custom-call(bf16[1,176,2048]{2,1,0:T(8,128)(2,1)S(1)} %get-tuple-element.12.refs_0_, bf16[1,176,2048]{2,1,0:T(8,128)(2,1)S(1)} %get-tuple-element.13.refs_1_, ...), custom_call_target="tpu_custom_call" | custom-call | tf_op jit(solution)/shard_map/pallas_call | solution.py:329

commit v4 on v3

--- a/solution.py
+++ b/solution.py
@@ -26,11 +26,11 @@
 def kernel(
     dims,
     order_hbm, plan_hbm, q_hbm, k_hbm, v_hbm, do_hbm,
-    attn_hbm, dq_hbm, dk_hbm, dv_hbm,
+    attn_hbm, dq_hbm, dk_out, dv_out,
     order_ref, plan_ref, q_in, q_send, q_got, do_got, k_in, v_in, kv_send, kv_all, bias,
-    attn_buf, dq_buf, dk_acc, dv_acc, g_send, g_got, dk_out, dv_out,
+    attn_buf, dq_buf, dk_acc, dv_acc, g_send, g_got,
     q_lsem, k_lsem, q_ssem, q_rsem, do_ssem, do_rsem, kv_ssem, kv_rsem, fw_ssem,
-    g_ssem, g_rsem, out_sem, grad_sem,
+    g_ssem, g_rsem, out_sem,
 ):
     S, C, TP, R, KR, KP, kl, group, CH, block_len = dims
     hd = HEAD_DIM
@@ -233,10 +233,6 @@
                 for cc in range(1, C):
                     total = total + g_got[g, cc * TP + u, kind].astype(F32)
                 out[:, 0, cols] = total[:KR]
-    dk_copy = pltpu.make_async_copy(dk_out, dk_hbm, grad_sem.at[0])
-    dv_copy = pltpu.make_async_copy(dv_out, dv_hbm, grad_sem.at[1])
-    dk_copy.start()
-    dv_copy.start()
 
     @pl.loop(0, TP)
     def _(u):
@@ -256,8 +252,6 @@
         do_copy(i).wait_send()
         for copy in out_copies(i):
             copy.wait()
-    dk_copy.wait()
-    dv_copy.wait()
 
 
 def write_out(*refs):
@@ -298,7 +292,7 @@
                 pltpu.VMEM((KR, 1, KW), F32),
             ),
             in_specs=[hbm] * 6,
-            out_specs=[anywhere] * 4,
+            out_specs=[anywhere] * 2 + [pl.BlockSpec(memory_space=pltpu.VMEM)] * 2,
             scratch_shapes=[
                 pltpu.SMEM(block_order.shape, jnp.int32),
                 pltpu.SMEM(plan.shape, jnp.int32),
@@ -317,10 +311,8 @@
                 pltpu.VMEM((hd, NB * KP), F32),
                 pltpu.VMEM((kl, NB, 2, KP, hd), BF16),
                 pltpu.VMEM((kl, NB, 2, KP, hd), BF16),
-                pltpu.VMEM((KR, 1, KW), F32),
-                pltpu.VMEM((KR, 1, KW), F32),
                 dma((chunks,)), dma((4,)), dma((chunks,)), dma((chunks,)), dma((chunks,)), dma((chunks,)),
-                dma((TP,)), dma((NB,)), dma((TP, C)), dma((kl, NB)), dma((kl, NB)), dma((2, chunks)), dma((2,)),
+                dma((TP,)), dma((NB,)), dma((TP, C)), dma((kl, NB)), dma((kl, NB)), dma((2, chunks)),
             ],
             compiler_params=pltpu.CompilerParams(
                 collective_id=0, has_side_effects=True, vmem_limit_bytes=56 * 1024 * 1024

time: 52.4 us -> 51.8 us (0.989)
  Pallas kernels: 51.6 us -> 51 us
    pallas_call x1, Pallas kernels: 50.4 us -> 49.8 us  [body(): pl.pallas_call(functools.partial(kernel, dims), out_shape=(pltpu.VMEM((1,...]
where the time goes in v4:
time: 51.8 us; the launch traced here: 51.7 us
  Pallas kernels  51 us (98%)
  between operations  0.64 us (1%)
    pallas_call x1, Pallas kernels, body(): pl.pallas_call(functools.partial(kernel, dims), out_shape=(pltpu.VMEM((1,...  49.8 us
    pallas_call x1, Pallas kernels, body(): pl.pallas_call(write_out, out_shape=tuple((jax.ShapeDtypeStruct(r.shape,...  1.24 us

profile of v4, /device:TPU:0, one launch (start us, length us, event | category | flops | bytes accessed | tf_op | source)
XLA Modules:
  0.0 51.7 jit_solution(9243020337317723007)
XLA Ops:
  0.6 49.8 %shard_map.93 = (bf16[1,176,2048]{2,1,0:T(8,128)(2,1)S(1)}, bf16[1,176,2048]{2,1,0:T(8,128)(2,1)S(1)}, f32[44,1,1024]{2,1,0:T(1,128)S(1)}, f32[44,1,1024]{2,1,0:T(1,128)S(1)}) custom-call(s32[4]{0:T(128)} %order_hbm.1, s32[4]{0:T(128)} %plan_hbm.1, bf16[1,2,176,2048]{3,2,1,0:T(8,128)(2,1)} %q_hbm.1, bf16[1,44,2,1024]{3,2,1,0:T(2,128)(2,1)} %bitcast.4, ...), custom_call_target="tpu_custom_call" | custom-call | tf_op jit(solution)/shard_map/pallas_call | solution.py:286
  50.4 1.2 %shard_map.94 = (bf16[1,176,2048]{2,1,0:T(8,128)(2,1)}, bf16[1,176,2048]{2,1,0:T(8,128)(2,1)}, f32[44,1,1024]{2,1,0:T(1,128)}, f32[44,1,1024]{2,1,0:T(1,128)}) custom-call(bf16[1,176,2048]{2,1,0:T(8,128)(2,1)S(1)} %get-tuple-element.12.refs_0_, bf16[1,176,2048]{2,1,0:T(8,128)(2,1)S(1)} %get-tuple-element.13.refs_1_, ...), custom_call_target="tpu_custom_call" | custom-call | tf_op jit(solution)/shard_map/pallas_call | solution.py:321
